TPU v7x, 128 devices: a whole 4x4x4 slice. The times are simulated.
128 devices in a mesh: var: 8 (over z, x_hi), patch: 8 (over y, core), win: 2 (over x_lo).
Axes of the slice: x: 4 (x_hi: 2, x_lo: 2; x = x_hi * 2 + x_lo), y: 4, z: 4, core: 2. Of those that a mesh axis runs over, the one named last changes fastest.
Arguments:
- fields: bfloat16 [480, 16, 1024], P(('win', 'var'), 'patch'), parts along dimension 0, may hold values from -6 to 6
- var_ids: int32 [240], replicated, may hold values from 0 to 239, each once
- level_of: int32 [240], replicated, may hold values from 0 to 37
- window_offset: int32 [2], P('win'), parts along dimension 0, may hold values from 0 to 164
- w_embed: bfloat16 [240, 16, 512], replicated, may hold values from -1.5 to 1.5
- var_emb: bfloat16 [240, 512], replicated, may hold values from -6 to 6
- w_key: bfloat16 [512, 512], replicated, may hold values from -0.25 to 0.25
- w_value: bfloat16 [512, 512], replicated, may hold values from -0.25 to 0.25
- w_out: bfloat16 [512, 512], replicated, may hold values from -0.25 to 0.25
- latent_query: float32 [8, 64], replicated, may hold values from -9 to 9
- bias_table: float32 [38, 8], replicated, may hold values from -4 to 300
- lat_emb: bfloat16 [180, 512], replicated, may hold values from -3 to 3
- d_aggregated: bfloat16 [32, 64, 512], P('win', ('var', 'patch')), parts along dimension 0, may hold values from -6 to 6
Outputs:
- aggregated: bfloat16 [32, 64, 512], P('win', ('var', 'patch')), parts along dimension 0
- embed_grad_rows: float32 [480, 16, 512], P(('win', 'var')), parts along dimension 0
- var_grad_rows: float32 [480, 512], P(('win', 'var')), parts along dimension 0
- key_grad: float32 [1024, 512], P('win'), parts along dimension 0
- value_grad: float32 [1024, 512], P('win'), parts along dimension 0
There are 2 independent parts, one for each index of `win`. A program takes and returns all parts, laid end to end along the dimension named above; an argument that names none is the same for every part. Nothing has to cross between parts.
All inputs are finite; a program needn't handle non-finite values.
Results may differ from a plain program's by a relative error of at most 0.017.
Values may be sent and summed in bfloat16 or wider, within the bound.
A program may use at most 128 MiB of HBM per device.

v0:
```python
import jax
import jax.numpy as jnp
from jax import lax
from jax.sharding import PartitionSpec as P


def attend(tokens, bias_rows, latent_query, w_key, w_value, w_out, lat_rows, cotangent):
    var_count, patch_count, width = tokens.shape
    head_count, head_size = latent_query.shape
    score_scale = head_size ** (-0.5)
    flat_tokens = tokens.reshape(var_count * patch_count, width)
    key_rows = jnp.dot(flat_tokens, w_key, preferred_element_type=jnp.float32)
    key_heads = key_rows.reshape(var_count, patch_count, head_count, head_size)
    inverse_rms = lax.rsqrt(jnp.mean(key_heads * key_heads, axis=-1, keepdims=True) + 1e-06)
    normed = key_heads * inverse_rms
    scores = (
        jnp.einsum("vphe,he->phv", normed, latent_query, precision=lax.Precision.HIGHEST)
        * score_scale
        + bias_rows.T[None]
    )
    largest = jnp.max(scores, axis=-1, keepdims=True)
    raised = jnp.exp(scores - largest)
    weights = raised / jnp.sum(raised, axis=-1, keepdims=True)
    attn_rounded = weights.astype(jnp.bfloat16)
    mixed_rows = jnp.einsum(
        "phv,vpd->phd", attn_rounded, tokens, preferred_element_type=jnp.float32
    ).astype(jnp.bfloat16)
    value_heads = w_value.reshape(width, head_count, head_size)
    context = (
        jnp.einsum("phd,dhe->phe", mixed_rows, value_heads, preferred_element_type=jnp.float32)
        .astype(jnp.bfloat16)
        .reshape(patch_count, width)
    )
    output = (jnp.dot(context, w_out, preferred_element_type=jnp.float32) + lat_rows).astype(
        jnp.bfloat16
    )
    grad_context = jnp.dot(cotangent, w_out.T, preferred_element_type=jnp.float32).astype(
        jnp.bfloat16
    )
    grad_heads = grad_context.reshape(patch_count, head_count, head_size)
    value_grad = jnp.einsum(
        "phd,phe->dhe", mixed_rows, grad_heads, preferred_element_type=jnp.float32
    ).reshape(width, width)
    grad_mixed = jnp.einsum(
        "phe,dhe->phd", grad_heads, value_heads, preferred_element_type=jnp.float32
    ).astype(jnp.bfloat16)
    grad_attn = jnp.einsum("phd,vpd->phv", grad_mixed, tokens, preferred_element_type=jnp.float32)
    grad_scores = weights * (grad_attn - jnp.sum(weights * grad_attn, axis=-1, keepdims=True))
    grad_normed = (
        jnp.einsum("phv,he->vphe", grad_scores, latent_query, precision=lax.Precision.HIGHEST)
        * score_scale
    )
    grad_keys = (
        inverse_rms
        * (grad_normed - normed * jnp.mean(grad_normed * normed, axis=-1, keepdims=True))
    ).astype(jnp.bfloat16)
    grad_keys = grad_keys.reshape(var_count * patch_count, width)
    key_grad = jnp.einsum("nd,ne->de", flat_tokens, grad_keys, preferred_element_type=jnp.float32)
    through_keys = jnp.dot(grad_keys, w_key.T, preferred_element_type=jnp.float32).reshape(
        var_count, patch_count, width
    )
    through_values = jnp.einsum(
        "phv,phd->vpd", attn_rounded, grad_mixed, preferred_element_type=jnp.float32
    )
    token_grad = (through_values + through_keys).astype(jnp.bfloat16)
    return (output, token_grad, key_grad, value_grad)


def embed_tokens(patches, w_rows, emb_rows):
    summed = jnp.einsum("vpk,vkd->vpd", patches, w_rows, preferred_element_type=jnp.float32)
    return (summed + emb_rows[:, None, :]).astype(jnp.bfloat16)


def local(
    fields,
    var_ids,
    level_of,
    window_offset,
    w_embed,
    var_emb,
    w_key,
    w_value,
    w_out,
    latent_query,
    bias_table,
    lat_emb,
    d_aggregated,
):
    local_vars, local_rows, merged = fields.shape
    pixels = w_embed.shape[1]
    width = w_embed.shape[2]
    row_count = d_aggregated.shape[0]
    own_cols = d_aggregated.shape[1]
    level_count = bias_table.shape[0]
    all_cols = merged // pixels
    var_devices = lax.axis_size("var")
    patch_devices = lax.axis_size("patch")
    levels = jnp.take(level_of, var_ids, axis=0)
    one_hot = (levels[:, None] == jnp.arange(level_count, dtype=jnp.int32)[None, :]).astype(
        jnp.float32
    )
    bias_rows = jnp.dot(one_hot, bias_table, precision=lax.Precision.HIGHEST)
    lat_slice = lax.dynamic_slice_in_dim(lat_emb, window_offset[0], row_count, 0)
    lat_rows = lat_slice[:, None, :].reshape(row_count * own_cols, width)
    cotangent = d_aggregated.reshape(row_count * own_cols, width)
    row_start = lax.axis_index("var") * local_vars
    local_ids = lax.dynamic_slice_in_dim(var_ids, row_start, local_vars, 0)
    w_rows = jnp.take(w_embed, local_ids, axis=0)
    emb_rows = jnp.take(var_emb, local_ids, axis=0)
    patches = fields.reshape(local_vars, local_rows * all_cols, pixels)
    local_tokens = embed_tokens(patches, w_rows, emb_rows).reshape(
        local_vars, local_rows, all_cols * width
    )
    owned_tokens = lax.all_to_all(
        lax.all_to_all(local_tokens, "var", split_axis=2, concat_axis=0, tiled=True),
        "patch",
        split_axis=2,
        concat_axis=1,
        tiled=True,
    )
    output, token_grad, key_grad, value_grad = attend(
        owned_tokens, bias_rows, latent_query, w_key, w_value, w_out, lat_rows, cotangent
    )
    returned = lax.all_to_all(
        lax.all_to_all(token_grad, "var", split_axis=0, concat_axis=2, tiled=True),
        "patch",
        split_axis=1,
        concat_axis=2,
        tiled=True,
    )
    returned = returned.reshape(
        local_vars, local_rows, patch_devices, var_devices, own_cols * width
    )
    local_grad = returned.transpose(0, 1, 3, 2, 4).reshape(local_vars, local_rows * all_cols, width)
    embed_part = jnp.einsum("vpk,vpd->vkd", patches, local_grad, preferred_element_type=jnp.float32)
    var_part = jnp.sum(local_grad, axis=1, dtype=jnp.float32)
    embed_grad, var_grad = (
        lax.psum(embed_part.astype(jnp.bfloat16), "patch").astype(jnp.float32),
        lax.psum(var_part.astype(jnp.bfloat16), "patch").astype(jnp.float32),
    )
    key_grad, value_grad = lax.psum((key_grad, value_grad), ("var", "patch"))
    return (output.reshape(row_count, own_cols, width), embed_grad, var_grad, key_grad, value_grad)


def solution(mesh):
    in_specs = (
        P(("win", "var"), "patch", None),
        P(),
        P(),
        P("win"),
        P(),
        P(),
        P(),
        P(),
        P(),
        P(),
        P(),
        P(),
        P("win", ("var", "patch"), None),
    )
    out_specs = (
        P("win", ("var", "patch"), None),
        P(("win", "var"), None, None),
        P(("win", "var"), None),
        P("win", None),
        P("win", None),
    )
    return jax.shard_map(local, mesh=mesh, in_specs=in_specs, out_specs=out_specs, check_vma=False)
```

profile of v0, /device:TPU:1, one launch (start us, length us, event | category | flops | bytes accessed | tf_op | source)
XLA Modules:
  0.0 1303.5 jit_solution(16177951120995973303)
XLA Ops:
  7.2 0.8 compare_and_fusion
  8.0 1.6 gather_fusion.1
  9.6 2.7 gather_fusion
  12.3 1.2 copy.91
  13.5 0.5 copy.92
  14.2 5.0 fusion.8
  19.2 6.3 copy.93
  25.4 9.9 reshape.98
  35.4 38.3 %copy.94 = bf16[30,2,32768]{0,1,2:T(2,128)(2,1)} copy(bf16[30,2,32768]{2,1,0:T(2,128)(2,1)} %reshape.98) | data formatting | bytes 7864320 | tf_op jit(solution)/shard_map/reshape | solution.py:111
  73.7 39.7 %reshape.143 = bf16[8,2,122880]{2,1,0:T(2,128)(2,1)} reshape(bf16[32768,2,30]{2,1,0:T(2,128)(2,1)} %bitcast.123) | data formatting | bytes 7864320
  113.4 56.1 %all_to_all.66 = bf16[8,2,122880]{2,1,0:T(2,128)(2,1)} all-to-all(bf16[8,2,122880]{2,1,0:T(2,128)(2,1)} %reshape.143), channel_id=1, replica_groups=mesh['var'=8,'patch'=8,'win'=2] {'var'}, dimensions={0} | all-to-all | bytes 7864320 | tf_op jit(solution)/shard_map/all_to_all | solution.py:115
  169.5 46.5 %reshape.144 = bf16[32768,2,30]{2,1,0:T(2,128)(2,1)} reshape(bf16[8,2,122880]{2,1,0:T(2,128)(2,1)} %all_to_all.66) | data formatting | bytes 7864320
  216.0 40.5 %copy.95 = bf16[30,2,8,4096]{3,1,0,2:T(2,128)(2,1)} copy(bf16[30,2,8,4096]{0,1,3,2:T(2,128)(2,1)} %bitcast.124) | data formatting | bytes 7864320 | tf_op jit(solution)/shard_map/all_to_all | solution.py:115
  256.6 14.9 %copy.96 = bf16[240,2,4096]{0,1,2:T(2,128)(2,1)} copy(bf16[240,2,4096]{2,1,0:T(2,128)(2,1)} %bitcast.132) | data formatting | bytes 7864320 | tf_op jit(solution)/shard_map/all_to_all | solution.py:115
  271.5 6.5 all-to-all-start.1
  278.4 0.2 convolution_convert_fusion.4
  278.8 1.9 gather_fusion.2
  280.8 0.2 convolution_bitcast_fusion
  281.0 0.3 fusion.13
  281.3 45.5 %all-to-all-done.1 = bf16[240,2,4096]{0,1,2:T(2,128)(2,1)} async-done(((bf16[240,2,4096]{0,1,2:T(2,128)(2,1)}), bf16[240,2,4096]{0,1,2:T(2,128)(2,1)}, u32[]{:S(2)}, u32[]{:S(2)}) %all-to-all-start.1) | async-done | bytes 3932192 | tf_op jit(solution)/shard_map/all_to_all | solution.py:114
  326.9 15.9 %copy.97 = bf16[240,2,8,512]{3,1,2,0:T(2,128)(2,1)} copy(bf16[240,2,8,512]{0,1,3,2:T(2,128)(2,1)} %bitcast.5) | data formatting | bytes 7864320 | tf_op jit(solution)/shard_map/all_to_all | solution.py:114
  342.7 9.1 reshape.136
  351.8 9.8 multiply_reduce_fusion
  361.8 11.1 copy.128
  372.8 6.8 broadcast_multiply_fusion
  379.6 33.2 %fusion.5 = f32[8,1,240,16]{2,1,3,0:T(1,128)S(1)} fusion(f32[8,64,1,1]{1,2,3,0:T(1,128)S(1)} %bitcast.140, f32[240,16,8,64]{3,1,2,0:T(8,128)S(1)} %broadcast_multiply_fusion), kind=kOutput, calls=%fused_computation.10 | convolution fusion | flops 23592960 | bytes 7989248 | tf_op jit(solution)/shard_map/vphe,he->phv/dot_general | solution.py:17
  412.9 0.3 fusion.46
  413.2 1.1 fusion.29
  414.3 1.2 fusion.17
  415.5 1.3 copy.107
  416.8 15.7 %fusion.2 = f32[240,16,8]{1,2,0:T(8,128)S(1)} fusion(f32[8,64]{1,0:T(8,128)S(1)} %copy-done.15, f32[8,16,240]{1,0,2:T(8,128)S(1)} %copy.107, f32[240,16,8,64]{3,1,2,0:T(8,128)} %get-tuple-element.10, f32[240,16,8]{1,2,0:T(8,128)S(1)} %add_rsqrt_fusion), kind=kLoop, calls=%fused_computation.7 | loop fusion | flops 9799680 | bytes 8235008 | tf_op jit(solution)/shard_map/reduce_sum | solution.py:55
  432.5 17.5 %fusion.4 = bf16[240,16,8,64]{3,1,2,0:T(8,128)(2,1)} fusion(f32[240,16,8]{1,2,0:T(8,128)S(1)} %broadcast_multiply_fusion.1, f32[8,64]{1,0:T(8,128)S(1)} %copy-done.15, f32[8,16,240]{1,0,2:T(8,128)S(1)} %copy.107, f32[240,16,8]{1,2,0:T(8,128)S(1)} %add_rsqrt_fusion, f32[240,16,8,64]{3,1,2,0:T(8,128)} %get-tuple-element.10), kind=kLoop, calls=%fused_computation.9 | loop fusion | flops 13762560 | bytes 12167168 | tf_op jit(solution)/shard_map/convert_element_type | solution.py:56
  450.0 10.4 copy.108
  460.4 4.7 fusion.21
  465.1 1.3 fusion.7
  466.5 2.2 copy.111
  468.7 49.6 %all_to_all.67 = bf16[240,16,512]{2,1,0:T(8,128)(2,1)S(1)} all-to-all(bf16[240,16,512]{2,1,0:T(8,128)(2,1)S(1)} %copy.111), channel_id=1, replica_groups=mesh['var'=8,'patch'=8,'win'=2] {'var'}, dimensions={0} | all-to-all | bytes 7864320 | tf_op jit(solution)/shard_map/all_to_all | solution.py:125
  518.3 4.2 copy.127
  522.5 6.4 reshape.142
  528.9 6.4 all-to-all-start.3
  535.5 10.3 copy.117
  545.8 9.1 reshape.106
  554.9 11.2 reshape.107
  566.1 2.9 convolution_convert_fusion.2
  569.0 0.4 copy-done.4
  569.4 5.3 fusion.47
  574.7 9.5 all-to-all-done.3
  584.2 4.3 copy.114
  588.6 1.8 copy-done.3
  590.4 1.4 fusion.11
  591.9 0.3 all-reduce.6.cloned.1.call-start
  592.2 0.3 fusion.32
  592.5 1.3 copy.120
  594.5 0.2 fusion.18
  594.9 1.5 fusion.20
  596.4 4.2 copy.131
  600.6 0.7 bitcast_reduce_fusion.1
  601.4 21.2 %psum.29 = bf16[30,512]{1,0:T(8,128)(2,1)S(1)} all-reduce(bf16[30,512]{1,0:T(8,128)(2,1)S(1)} %bitcast_reduce_fusion.1), channel_id=1, replica_groups=mesh['var'=8,'patch'=8,'win'=2] {'patch'}, use_global_device_ids=true, to_apply=%region_7.8 | all-reduce | flops 15360 | bytes 61440 | tf_op jit(solution)/shard_map/psum | solution.py:139
  622.5 0.6 convert_element_type.79
  623.2 23.5 %all-reduce.4.cloned.1.call-done = bf16[30,16,512]{2,1,0:T(8,128)(2,1)} async-done(((bf16[30,16,512]{2,1,0:T(8,128)(2,1)}), bf16[30,16,512]{2,1,0:T(8,128)(2,1)}) %all-reduce.4.cloned.1.call-update) | async-done | bytes 491536 | tf_op jit(solution)/shard_map/psum | solution.py:138
  646.6 2.1 convert_element_type.78
  648.7 643.1 %all-reduce.6.cloned.1.call-done = (f32[512,512]{1,0:T(8,128)}, f32[512,512]{1,0:T(8,128)}) async-done(((f32[512,512]{1,0:T(8,128)}, f32[512,512]{1,0:T(8,128)}), (f32[512,512]{1,0:T(8,128)}, f32[512,512]{1,0:T(8,128)})) %all-reduce.6.cloned.1.call-update) | async-done | bytes 2097168 | tf_op jit(solution)/shard_map/psum | solution.py:141
  1291.8 2.3 copy.159
  1294.1 2.3 copy.160
  (51 shorter events, 1.3 us)
Async XLA Ops:
  7.2 271.2 %copy-start = (bf16[512,512]{1,0:T(8,128)(2,1)S(1)}, bf16[512,512]{1,0:T(8,128)(2,1)}, u32[]{:S(2)}) copy-start(bf16[512,512]{1,0:T(8,128)(2,1)} %param.21) | copy-start | bytes 1572868
  14.1 11.4 copy-start.10
  271.4 6.5 copy-start.5
  271.4 6.7 copy-start.12
  271.4 7.0 copy-start.16
  271.4 7.3 copy-start.17
  271.5 7.4 copy-start.1
  271.5 9.3 copy-start.18
  271.5 55.4 %all-to-all-start.1 = ((bf16[240,2,4096]{0,1,2:T(2,128)(2,1)}), bf16[240,2,4096]{0,1,2:T(2,128)(2,1)}, u32[]{:S(2)}, u32[]{:S(2)}) async-start(bf16[240,2,4096]{0,1,2:T(2,128)(2,1)} %copy.96), calls=%async_computation.1 | async-start | bytes 8388608 | tf_op jit(solution)/shard_map/all_to_all | solution.py:114
  278.8 64.0 %copy-start.13 = (bf16[16,8,64]{2,1,0:T(8,128)(2,1)}, bf16[16,8,64]{2,1,0:T(8,128)(2,1)S(1)}, u32[]{:S(2)}) copy-start(bf16[16,8,64]{2,1,0:T(8,128)(2,1)S(1)} %reshape.103) | copy-start | bytes 49156
  281.3 131.8 %copy-start.8 = (bf16[16,8,512]{2,0,1:T(8,128)(2,1)}, bf16[16,8,512]{2,0,1:T(8,128)(2,1)S(1)}, u32[]{:S(2)}) copy-start(bf16[16,8,512]{2,0,1:T(8,128)(2,1)S(1)} %fusion.13) | copy-start | bytes 393220
  372.8 6.8 copy-start.15
  379.6 33.5 %copy-start.2 = (bf16[240,8,2,512]{3,0,2,1:T(8,128)(2,1)S(1)}, bf16[240,8,2,512]{3,0,2,1:T(8,128)(2,1)}, u32[]{:S(2)}) copy-start(bf16[240,8,2,512]{3,0,2,1:T(8,128)(2,1)} %copy.128) | copy-start | bytes 11796484
  413.1 1.1 copy-start.6
  460.4 4.7 copy-start.7
  460.4 4.7 copy-start.9
  528.9 55.3 %all-to-all-start.3 = ((bf16[30,16,4096]{2,0,1:T(8,128)(2,1)}), bf16[30,16,4096]{2,0,1:T(8,128)(2,1)}, u32[]{:S(2)}, u32[]{:S(2)}) async-start(bf16[30,16,4096]{2,0,1:T(8,128)(2,1)} %reshape.142), calls=%async_computation.3 | async-start | bytes 8388608 | tf_op jit(solution)/shard_map/all_to_all | solution.py:124
  535.3 111.3 %all-reduce.4.cloned.1.call-start = ((), (), s32[]{:S(2)}) async-start(), calls=%async_computation.4 | async-start | bytes 983040 | tf_op jit(solution)/shard_map/psum | solution.py:138
  566.1 3.3 copy-start.4
  574.7 15.8 %copy-start.11 = (bf16[30,128,16]{1,2,0:T(8,128)(2,1)S(1)}, bf16[30,128,16]{1,2,0:T(8,128)(2,1)}, u32[]{:S(2)}) copy-start(bf16[30,128,16]{1,2,0:T(8,128)(2,1)} %copy-done.10) | copy-start | bytes 368644
  588.5 1.9 copy-start.3
  588.6 3.6 copy-start.14
  591.9 700.0 %all-reduce.6.cloned.1.call-start = ((), (), s32[]{:S(2)}) async-start(), calls=%async_computation.5 | async-start | bytes 4194304 | tf_op jit(solution)/shard_map/psum | solution.py:141
Sparse Core Ops, SparseCore 0:
  592.0 54.5 all-reduce.3
  649.8 641.9 all-reduce.5
where the time goes:
time: 1320 us; the launch traced here: 1300 us
  waiting for transfers between devices  722 us (55%)
  local copies, waits for them, and re-layouts  313 us (24%)
  blocking collectives  127 us (10%)
  matrix products  67.6 us (5%)
  other arithmetic  46 us (3%)
  between operations  15.3 us (1%)
  starting transfers between devices  13.4 us (1%)
    psum x1, waiting for transfers between devices, local(): key_grad, value_grad = lax.psum((key_grad, value_grad), ('var', 'patch'))  643 us
    unnamed x46, local copies, waits for them, and re-layouts  98.9 us
    all_to_all x1, blocking collectives, local(): lax.all_to_all(local_tokens, 'var', split_axis=2, concat_axis=0, tiled=True)  56.1 us
    all_to_all x2, local copies, waits for them, and re-layouts, local(): lax.all_to_all(local_tokens, 'var', split_axis=2, concat_axis=0, tiled=True)  55.4 us
    all_to_all x1, blocking collectives, local(): lax.all_to_all(token_grad, 'var', split_axis=0, concat_axis=2, tiled=True)  49.6 us
    reshape x2, local copies, waits for them, and re-layouts, local(): embed_tokens(patches, w_rows, emb_rows)  48.2 us
    all_to_all x1, waiting for transfers between devices, local(): lax.all_to_all(lax.all_to_all(local_tokens, 'var', split_axis=2, concat_a...  45.5 us
    dot_general x1, matrix products, attend(): jnp.einsum('vphe,he->phv', normed, latent_query, precision=lax.Precision....  33.2 us
  transfers between devices with their start and end apart: 4, of which 4 were waited for; matrix products, arithmetic and copies ran while one was open for 4% of the time, Pallas kernels for 0%

commit v1 on v0

--- a/solution.py
+++ b/solution.py
@@ -138,7 +138,10 @@
         lax.psum(embed_part.astype(jnp.bfloat16), "patch").astype(jnp.float32),
         lax.psum(var_part.astype(jnp.bfloat16), "patch").astype(jnp.float32),
     )
-    key_grad, value_grad = lax.psum((key_grad, value_grad), ("var", "patch"))
+    open_windows_all = lambda content, dev_axis, chip_axis: lax.psum(
+        lax.psum(content, dev_axis), chip_axis
+    )
+    key_grad, value_grad = open_windows_all((key_grad, value_grad), "var", "patch")
     return (output.reshape(row_count, own_cols, width), embed_grad, var_grad, key_grad, value_grad)
 
 

time: 1320 us -> 836 us (0.63)
  waiting for transfers between devices: 722 us -> 238 us
    psum x1 -> x2, waiting for transfers between devices: 643 us -> 156 us  [the longest x1 90.4 us: local(): lax.psum(content, dev_axis)]
    unnamed x46 -> x44, local copies, waits for them, and re-layouts: 98.9 us -> 98.5 us
  transfers between devices with their start and end apart: 4 -> 5, of which waited for: 4 -> 5; matrix products, arithmetic and copies ran while one was open for 4% -> 7% of each run, Pallas kernels for 0% -> 0%
where the time goes in v1:
time: 836 us; the launch traced here: 822 us
  local copies, waits for them, and re-layouts  312 us (37%)
  waiting for transfers between devices  238 us (28%)
  blocking collectives  128 us (15%)
  matrix products  68.8 us (8%)
  other arithmetic  46 us (6%)
  between operations  15 us (2%)
  starting transfers between devices  13.4 us (2%)
    unnamed x44, local copies, waits for them, and re-layouts  98.5 us
    psum x1, waiting for transfers between devices, local(): lax.psum(content, dev_axis)  90.4 us
    psum x1, waiting for transfers between devices, local(): lax.psum(lax.psum(content, dev_axis), chip_axis)  65.8 us
    all_to_all x1, blocking collectives, local(): lax.all_to_all(local_tokens, 'var', split_axis=2, concat_axis=0, tiled=True)  56.1 us
    all_to_all x2, local copies, waits for them, and re-layouts, local(): lax.all_to_all(local_tokens, 'var', split_axis=2, concat_axis=0, tiled=True)  55.4 us
    all_to_all x1, blocking collectives, local(): lax.all_to_all(token_grad, 'var', split_axis=0, concat_axis=2, tiled=True)  49.6 us
    reshape x2, local copies, waits for them, and re-layouts, local(): embed_tokens(patches, w_rows, emb_rows)  48.4 us
    all_to_all x1, waiting for transfers between devices, local(): lax.all_to_all(lax.all_to_all(local_tokens, 'var', split_axis=2, concat_a...  45.5 us
  transfers between devices with their start and end apart: 5, of which 5 were waited for; matrix products, arithmetic and copies ran while one was open for 7% of the time, Pallas kernels for 0%

profile of v1, /device:TPU:1, one launch (start us, length us, event | category | flops | bytes accessed | tf_op | source)
XLA Modules:
  0.0 821.7 jit_solution(7448198468845450934)
XLA Ops:
  7.2 0.8 compare_and_fusion
  8.0 1.6 gather_fusion.1
  9.6 2.7 gather_fusion
  12.3 1.2 copy.91
  13.5 0.5 copy.92
  14.2 5.0 fusion.8
  19.2 6.3 copy.93
  25.5 9.9 %reshape.98 = bf16[30,2,32768]{2,1,0:T(2,128)(2,1)} reshape(bf16[30,128,512]{2,1,0:T(8,128)(2,1)} %copy.93) | data formatting | bytes 7864320 | tf_op jit(solution)/shard_map/reshape | solution.py:111
  35.4 38.4 %copy.94 = bf16[30,2,32768]{0,1,2:T(2,128)(2,1)} copy(bf16[30,2,32768]{2,1,0:T(2,128)(2,1)} %reshape.98) | data formatting | bytes 7864320 | tf_op jit(solution)/shard_map/reshape | solution.py:111
  73.8 39.8 %reshape.143 = bf16[8,2,122880]{2,1,0:T(2,128)(2,1)} reshape(bf16[32768,2,30]{2,1,0:T(2,128)(2,1)} %bitcast.123) | data formatting | bytes 7864320
  113.6 56.1 %all_to_all.66 = bf16[8,2,122880]{2,1,0:T(2,128)(2,1)} all-to-all(bf16[8,2,122880]{2,1,0:T(2,128)(2,1)} %reshape.143), channel_id=1, replica_groups=mesh['var'=8,'patch'=8,'win'=2] {'var'}, dimensions={0} | all-to-all | bytes 7864320 | tf_op jit(solution)/shard_map/all_to_all | solution.py:115
  169.7 46.5 %reshape.144 = bf16[32768,2,30]{2,1,0:T(2,128)(2,1)} reshape(bf16[8,2,122880]{2,1,0:T(2,128)(2,1)} %all_to_all.66) | data formatting | bytes 7864320
  216.2 40.5 %copy.95 = bf16[30,2,8,4096]{3,1,0,2:T(2,128)(2,1)} copy(bf16[30,2,8,4096]{0,1,3,2:T(2,128)(2,1)} %bitcast.124) | data formatting | bytes 7864320 | tf_op jit(solution)/shard_map/all_to_all | solution.py:115
  256.7 14.9 %copy.96 = bf16[240,2,4096]{0,1,2:T(2,128)(2,1)} copy(bf16[240,2,4096]{2,1,0:T(2,128)(2,1)} %bitcast.132) | data formatting | bytes 7864320 | tf_op jit(solution)/shard_map/all_to_all | solution.py:115
  271.6 6.5 all-to-all-start.1
  278.6 0.2 convolution_convert_fusion.4
  279.0 1.9 gather_fusion.2
  281.0 0.2 convolution_bitcast_fusion
  281.2 0.3 fusion.13
  281.5 45.5 %all-to-all-done.1 = bf16[240,2,4096]{0,1,2:T(2,128)(2,1)} async-done(((bf16[240,2,4096]{0,1,2:T(2,128)(2,1)}), bf16[240,2,4096]{0,1,2:T(2,128)(2,1)}, u32[]{:S(2)}, u32[]{:S(2)}) %all-to-all-start.1) | async-done | bytes 3932192 | tf_op jit(solution)/shard_map/all_to_all | solution.py:114
  327.0 15.8 %copy.97 = bf16[240,2,8,512]{3,1,2,0:T(2,128)(2,1)} copy(bf16[240,2,8,512]{0,1,3,2:T(2,128)(2,1)} %bitcast.5) | data formatting | bytes 7864320 | tf_op jit(solution)/shard_map/all_to_all | solution.py:114
  342.9 9.1 %reshape.136 = bf16[240,16,512,1]{2,1,0,3:T(8,128)(2,1)} reshape(bf16[240,8,2,512]{3,2,1,0:T(2,128)(2,1)} %bitcast.125) | data formatting | bytes 7864320 | tf_op jit(solution)/shard_map/dot_general | solution.py:12
  352.0 9.8 %multiply_reduce_fusion = (f32[240,16,8]{1,2,0:T(8,128)S(1)}, f32[240,16,8,64]{3,1,2,0:T(8,128)}) fusion(bf16[8,64,512,1]{2,1,0,3:T(8,128)(2,1)S(1)} %bitcast.139, bf16[240,16,512,1]{2,1,0,3:T(8,128)(2,1)} %reshape.136), kind=kOutput, calls=%fused_computation.13 | convolution fusion | flops 2017167360 | bytes 12443648 | tf_op jit(solution)/shard_map/dot_general | solution.py:12
  361.9 11.1 %copy.128 = bf16[240,8,2,512]{3,0,2,1:T(8,128)(2,1)} copy(bf16[240,8,2,512]{0,2,3,1:T(2,128)(2,1)} %bitcast.41) | data formatting | bytes 7864320 | tf_op jit(solution)/shard_map/dot_general | solution.py:12
  373.0 6.8 broadcast_multiply_fusion
  379.8 33.2 %fusion.5 = f32[8,1,240,16]{2,1,3,0:T(1,128)S(1)} fusion(f32[8,64,1,1]{1,2,3,0:T(1,128)S(1)} %bitcast.140, f32[240,16,8,64]{3,1,2,0:T(8,128)S(1)} %broadcast_multiply_fusion), kind=kOutput, calls=%fused_computation.10 | convolution fusion | flops 23592960 | bytes 7989248 | tf_op jit(solution)/shard_map/vphe,he->phv/dot_general | solution.py:17
  413.0 0.3 fusion.46
  413.3 1.1 fusion.29
  414.4 1.2 fusion.17
  415.6 1.3 copy.107
  416.9 15.7 %fusion.2 = f32[240,16,8]{1,2,0:T(8,128)S(1)} fusion(f32[8,64]{1,0:T(8,128)S(1)} %copy-done.14, f32[8,16,240]{1,0,2:T(8,128)S(1)} %copy.107, f32[240,16,8,64]{3,1,2,0:T(8,128)} %get-tuple-element.12, f32[240,16,8]{1,2,0:T(8,128)S(1)} %add_rsqrt_fusion), kind=kLoop, calls=%fused_computation.7 | loop fusion | flops 9799680 | bytes 8235008 | tf_op jit(solution)/shard_map/reduce_sum | solution.py:55
  432.7 17.5 %fusion.4 = bf16[240,16,8,64]{3,1,2,0:T(8,128)(2,1)} fusion(f32[240,16,8]{1,2,0:T(8,128)S(1)} %broadcast_multiply_fusion.1, f32[8,64]{1,0:T(8,128)S(1)} %copy-done.14, f32[8,16,240]{1,0,2:T(8,128)S(1)} %copy.107, f32[240,16,8]{1,2,0:T(8,128)S(1)} %add_rsqrt_fusion, f32[240,16,8,64]{3,1,2,0:T(8,128)} %get-tuple-element.12), kind=kLoop, calls=%fused_computation.9 | loop fusion | flops 13762560 | bytes 12167168 | tf_op jit(solution)/shard_map/convert_element_type | solution.py:56
  450.2 10.4 %copy.108 = bf16[240,16,8,64]{0,3,2,1:T(8,128)(2,1)} copy(bf16[240,16,8,64]{3,1,2,0:T(8,128)(2,1)} %fusion.4) | data formatting | bytes 7864320 | tf_op jit(solution)/shard_map/convert_element_type | solution.py:56
  460.6 4.7 fusion.21
  465.3 1.3 fusion.7
  466.7 2.2 copy.111
  468.9 49.6 %all_to_all.67 = bf16[240,16,512]{2,1,0:T(8,128)(2,1)S(1)} all-to-all(bf16[240,16,512]{2,1,0:T(8,128)(2,1)S(1)} %copy.111), channel_id=1, replica_groups=mesh['var'=8,'patch'=8,'win'=2] {'var'}, dimensions={0} | all-to-all | bytes 7864320 | tf_op jit(solution)/shard_map/all_to_all | solution.py:125
  518.5 4.2 copy.127
  522.7 6.4 reshape.142
  529.1 6.4 all-to-all-start.3
  535.7 10.3 %copy.117 = bf16[240,16,8,64]{3,2,1,0:T(8,128)(2,1)} copy(bf16[240,16,8,64]{3,1,2,0:T(8,128)(2,1)} %fusion.4) | data formatting | bytes 7864320 | tf_op jit(solution)/shard_map/convert_element_type | solution.py:56
  546.0 9.1 %reshape.106 = bf16[3840,512]{1,0:T(8,128)(2,1)} reshape(bf16[240,8,2,512]{3,2,1,0:T(2,128)(2,1)} %bitcast.126) | data formatting | bytes 7864320 | tf_op jit(solution)/shard_map/reshape | solution.py:11
  555.0 11.2 %reshape.107 = bf16[3840,512]{1,0:T(8,128)(2,1)} reshape(bf16[240,16,8,64]{3,2,1,0:T(8,128)(2,1)} %copy.117) | data formatting | bytes 7864320 | tf_op jit(solution)/shard_map/reshape | solution.py:57
  566.3 2.8 convolution_convert_fusion.2
  569.0 0.4 fusion.32
  569.4 1.3 copy.120
  570.7 6.5 fusion.47
  577.3 7.1 all-to-all-done.3
  584.4 4.4 copy.114
  588.8 1.9 copy-done.2
  590.6 1.4 fusion.11
  592.1 0.3 all-reduce.8.cloned.1.call-start
  592.4 90.4 %all-reduce.10.cloned.1.call-done = (f32[512,512]{1,0:T(8,128)}, f32[512,512]{1,0:T(8,128)}) async-done(((f32[512,512]{1,0:T(8,128)}, f32[512,512]{1,0:T(8,128)}), (f32[512,512]{1,0:T(8,128)}, f32[512,512]{1,0:T(8,128)})) %all-reduce.10.cloned.1.call-update) | async-done | bytes 2097168 | tf_op jit(solution)/shard_map/psum | solution.py:142
  683.4 0.2 fusion.18
  683.8 1.5 fusion.20
  685.3 4.2 copy.131
  689.5 0.7 bitcast_reduce_fusion.1
  690.3 22.8 %psum.43 = bf16[30,512]{1,0:T(8,128)(2,1)S(1)} all-reduce(bf16[30,512]{1,0:T(8,128)(2,1)S(1)} %bitcast_reduce_fusion.1), channel_id=1, replica_groups=mesh['var'=8,'patch'=8,'win'=2] {'patch'}, use_global_device_ids=true, to_apply=%region_7.8 | all-reduce | flops 15360 | bytes 61440 | tf_op jit(solution)/shard_map/psum | solution.py:139
  713.0 0.6 convert_element_type.79
  713.7 28.8 %all-reduce.6.cloned.1.call-done = bf16[30,16,512]{2,1,0:T(8,128)(2,1)} async-done(((bf16[30,16,512]{2,1,0:T(8,128)(2,1)}), bf16[30,16,512]{2,1,0:T(8,128)(2,1)}) %all-reduce.6.cloned.1.call-update) | async-done | bytes 491536 | tf_op jit(solution)/shard_map/psum | solution.py:138
  742.4 2.1 convert_element_type.78
  744.5 65.8 %all-reduce.8.cloned.1.call-done = (f32[512,512]{1,0:T(8,128)}, f32[512,512]{1,0:T(8,128)}) async-done(((f32[512,512]{1,0:T(8,128)}, f32[512,512]{1,0:T(8,128)}), (f32[512,512]{1,0:T(8,128)}, f32[512,512]{1,0:T(8,128)})) %all-reduce.8.cloned.1.call-update) | async-done | bytes 2097168 | tf_op jit(solution)/shard_map/psum | solution.py:141
  810.3 2.3 copy.161
  812.6 2.3 copy.162
  (52 shorter events, 1.4 us)
Async XLA Ops:
  7.2 271.4 %copy-start = (bf16[512,512]{1,0:T(8,128)(2,1)S(1)}, bf16[512,512]{1,0:T(8,128)(2,1)}, u32[]{:S(2)}) copy-start(bf16[512,512]{1,0:T(8,128)(2,1)} %param.21) | copy-start | bytes 1572868
  14.1 11.4 %copy-start.9 = (bf16[30,128,16]{1,2,0:T(8,128)(2,1)}, bf16[30,128,16]{1,2,0:T(8,128)(2,1)S(1)}, u32[]{:S(2)}) copy-start(bf16[30,128,16]{1,2,0:T(8,128)(2,1)S(1)} %copy.92) | copy-start | bytes 368644
  271.6 6.5 copy-start.4
  271.6 6.7 copy-start.11
  271.6 7.0 copy-start.15
  271.6 7.3 copy-start.16
  271.6 7.4 copy-start.1
  271.6 9.3 %copy-start.17 = (f32[38,8]{0,1:T(8,128)S(1)}, f32[38,8]{0,1:T(8,128)}, u32[]{:S(2)}) copy-start(f32[38,8]{0,1:T(8,128)} %param.23) | copy-start | bytes 3652
  271.6 55.4 %all-to-all-start.1 = ((bf16[240,2,4096]{0,1,2:T(2,128)(2,1)}), bf16[240,2,4096]{0,1,2:T(2,128)(2,1)}, u32[]{:S(2)}, u32[]{:S(2)}) async-start(bf16[240,2,4096]{0,1,2:T(2,128)(2,1)} %copy.96), calls=%async_computation.1 | async-start | bytes 8388608 | tf_op jit(solution)/shard_map/all_to_all | solution.py:114
  279.0 63.9 %copy-start.12 = (bf16[16,8,64]{2,1,0:T(8,128)(2,1)}, bf16[16,8,64]{2,1,0:T(8,128)(2,1)S(1)}, u32[]{:S(2)}) copy-start(bf16[16,8,64]{2,1,0:T(8,128)(2,1)S(1)} %reshape.103) | copy-start | bytes 49156
  281.5 131.8 %copy-start.7 = (bf16[16,8,512]{2,0,1:T(8,128)(2,1)}, bf16[16,8,512]{2,0,1:T(8,128)(2,1)S(1)}, u32[]{:S(2)}) copy-start(bf16[16,8,512]{2,0,1:T(8,128)(2,1)S(1)} %fusion.13) | copy-start | bytes 393220
  373.0 6.8 copy-start.14
  379.8 33.5 %copy-start.3 = (bf16[240,8,2,512]{3,0,2,1:T(8,128)(2,1)S(1)}, bf16[240,8,2,512]{3,0,2,1:T(8,128)(2,1)}, u32[]{:S(2)}) copy-start(bf16[240,8,2,512]{3,0,2,1:T(8,128)(2,1)} %copy.128) | copy-start | bytes 11796484
  413.3 1.1 copy-start.5
  460.6 4.7 copy-start.6
  460.6 4.7 copy-start.8
  529.1 55.3 %all-to-all-start.3 = ((bf16[30,16,4096]{2,0,1:T(8,128)(2,1)}), bf16[30,16,4096]{2,0,1:T(8,128)(2,1)}, u32[]{:S(2)}, u32[]{:S(2)}) async-start(bf16[30,16,4096]{2,0,1:T(8,128)(2,1)} %reshape.142), calls=%async_computation.3 | async-start | bytes 8388608 | tf_op jit(solution)/shard_map/all_to_all | solution.py:124
  535.5 147.3 %all-reduce.10.cloned.1.call-start = ((), (), s32[]{:S(2)}) async-start(), calls=%async_computation.6 | async-start | bytes 4194304 | tf_op jit(solution)/shard_map/psum | solution.py:142
  566.3 2.8 copy-start.13
  577.3 13.3 %copy-start.10 = (bf16[30,128,16]{1,2,0:T(8,128)(2,1)S(1)}, bf16[30,128,16]{1,2,0:T(8,128)(2,1)}, u32[]{:S(2)}) copy-start(bf16[30,128,16]{1,2,0:T(8,128)(2,1)} %copy-done.9) | copy-start | bytes 368644
  577.3 165.2 %all-reduce.6.cloned.1.call-start = ((), (), s32[]{:S(2)}) async-start(), calls=%async_computation.4 | async-start | bytes 983040 | tf_op jit(solution)/shard_map/psum | solution.py:138
  588.8 1.9 copy-start.2
  592.1 218.3 %all-reduce.8.cloned.1.call-start = ((), (), s32[]{:S(2)}) async-start(), calls=%async_computation.5 | async-start | bytes 4194304 | tf_op jit(solution)/shard_map/psum | solution.py:141
Sparse Core Ops, SparseCore 0:
  577.4 105.2 all-reduce.9
  685.7 56.7 all-reduce.5
  745.0 65.2 all-reduce.7
